TPU v7x, 32 devices: a whole 2x2x4 slice. The times are simulated.
32 devices in a mesh: token: 4 (over z), head: 4 (over x, core), image: 2 (over y).
Axes of the slice: x: 2, y: 2, z: 4, core: 2. Of those that a mesh axis runs over, the one named last changes fastest.
Arguments:
- queries: bfloat16 [32, 80, 2048], P(('image', 'head'), None, 'token'), parts along dimension 0, may hold values from -6 to 6
- keys: bfloat16 [32, 80, 2048], P(('image', 'head'), None, 'token'), parts along dimension 0, may hold values from -6 to 6
- values: bfloat16 [32, 80, 2048], P(('image', 'head'), None, 'token'), parts along dimension 0, may hold values from -6 to 6
- out_grad: bfloat16 [32, 80, 2048], P(('image', 'head'), None, 'token'), parts along dimension 0, may hold values from -6 to 6
- flags: int32 [4, 4], replicated, may hold values from 0 to 1, as said below
- order: int32 [4], replicated, may hold values from 0 to 3, each once
Outputs:
- attended: bfloat16 [32, 80, 2048], P(('image', 'head'), None, 'token'), parts along dimension 0
- query_grad: bfloat16 [32, 80, 2048], P(('image', 'head'), None, 'token'), parts along dimension 0
- key_grad: bfloat16 [32, 80, 2048], P(('image', 'head'), None, 'token'), parts along dimension 0
- value_grad: bfloat16 [32, 80, 2048], P(('image', 'head'), None, 'token'), parts along dimension 0
There are 2 independent parts, one for each index of `image`. A program takes and returns all parts, laid end to end along the dimension named above; an argument that names none is the same for every part. Nothing has to cross between parts.
Inputs may be any that keep to these rules, and one draw needn't show every extreme that they name: `flags`: every image block may attend to itself. `order`: each image block once.
All inputs are finite; a program needn't handle non-finite values.
Results may differ from a plain program's by a relative error of at most 0.017.
Values may be sent and summed in bfloat16 or wider, within the bound.
A program may use at most 64 MiB of HBM per device.

v0:
```python
import jax
import jax.numpy as jnp
from jax import lax
from jax.sharding import PartitionSpec as P

BLK = 512


def from_behind(value, axis, steps):
    count = lax.axis_size(axis)
    pairs = [(source, (source + steps) % count) for source in range(count)]
    return lax.ppermute(value, axis, pairs)


def block_pairs(flags, order, query_dev, key_dev, per):
    nblk = order.shape[0]
    labels = jnp.arange(nblk, dtype=jnp.int32)[None, :]
    query_ids = lax.dynamic_slice_in_dim(order, query_dev * per, per)
    key_ids = lax.dynamic_slice_in_dim(order, key_dev * per, per)
    query_hot = (query_ids[:, None] == labels).astype(jnp.float32)
    key_hot = (key_ids[:, None] == labels).astype(jnp.float32)
    return jnp.dot(jnp.dot(query_hot, flags.astype(jnp.float32)), key_hot.T) > 0.5


def masked_scores(query, key, pairs, scale):
    score = jnp.einsum("hdi,hdj->hij", query, key, preferred_element_type=jnp.float32) * scale
    heads, rows, cols = score.shape
    per = pairs.shape[0]
    shaped = score.reshape(heads, per, rows // per, per, cols // per)
    shaped = jnp.where(pairs[None, :, None, :, None], shaped, -jnp.inf)
    return shaped.reshape(heads, rows, cols)


def forward_tile(query, key, value, state, pairs, scale):
    output, running_max, total = state
    score = masked_scores(query, key, pairs, scale)
    new_max = jnp.maximum(running_max, jnp.max(score, axis=2))
    safe_max = jnp.where(jnp.isfinite(new_max), new_max, 0.0)
    rescale = jnp.exp(running_max - safe_max)
    weight = jnp.exp(score - safe_max[..., None])
    total = total * rescale + jnp.sum(weight, axis=2)
    output = output * rescale[:, None, :] + jnp.einsum(
        "hij,hdj->hdi", weight.astype(jnp.bfloat16), value, preferred_element_type=jnp.float32
    )
    return (output, new_max, total)


def backward_tile(query, grad, lse, delta, key, value, pairs, scale):
    score = masked_scores(query, key, pairs, scale)
    prob = jnp.exp(score - lse[..., None])
    value_part = jnp.einsum(
        "hij,hdi->hdj", prob.astype(jnp.bfloat16), grad, preferred_element_type=jnp.float32
    )
    dprob = jnp.einsum("hdi,hdj->hij", grad, value, preferred_element_type=jnp.float32)
    dscore = (prob * (dprob - delta[..., None]) * scale).astype(jnp.bfloat16)
    key_part = jnp.einsum("hij,hdi->hdj", dscore, query, preferred_element_type=jnp.float32)
    query_part = jnp.einsum("hij,hdj->hdi", dscore, key, preferred_element_type=jnp.float32)
    return (query_part, key_part, value_part)


def body(queries, keys, values, out_grad, flags, order):
    cycle = lax.axis_size("token")
    me = lax.axis_index("token")
    heads, dim, toks = queries.shape
    per = toks // BLK
    scale = dim ** (-0.5)
    zero_field = jnp.zeros((heads, dim, toks), jnp.float32)
    zero_rows = jnp.zeros((heads, toks), jnp.float32)
    start_max = jnp.full((heads, toks), -jnp.inf, jnp.float32)

    def forward_step(step, carry):
        visitor, output, running_max, total = carry
        source = (me - step) % cycle
        pairs = block_pairs(flags, order, source, me, per)
        state = lax.cond(
            jnp.any(pairs),
            lambda s: forward_tile(visitor, keys, values, s, pairs, scale),
            lambda s: s,
            (output, running_max, total),
        )
        visitor = from_behind(visitor, "token", 1)
        output, running_max, total = from_behind(state, "token", 1)
        return (visitor, output, running_max, total)

    _, output, running_max, total = lax.fori_loop(
        0, cycle, forward_step, (queries, zero_field, start_max, zero_rows)
    )
    state = (output, running_max, total)
    finish_output, finish_running_max, finish_total = state
    attended = (finish_output / finish_total[:, None, :]).astype(jnp.bfloat16)
    lse = finish_running_max + jnp.log(finish_total)
    delta = jnp.sum(out_grad.astype(jnp.float32) * attended.astype(jnp.float32), axis=1)
    attended, lse, delta = (attended, lse, delta)

    def backward_step(step, carry):
        visitor, grad, query_acc, lse_vis, delta_vis, key_acc, value_acc = carry
        source = (me - step) % cycle
        pairs = block_pairs(flags, order, source, me, per)

        def live(accs):
            query_part, key_part, value_part = backward_tile(
                visitor, grad, lse_vis, delta_vis, keys, values, pairs, scale
            )
            return (accs[0] + query_part, accs[1] + key_part, accs[2] + value_part)

        query_acc, key_acc, value_acc = lax.cond(
            jnp.any(pairs), live, lambda a: a, (query_acc, key_acc, value_acc)
        )
        visitor, grad = from_behind((visitor, grad), "token", 1)
        query_acc, lse_vis, delta_vis = from_behind((query_acc, lse_vis, delta_vis), "token", 1)
        return (visitor, grad, query_acc, lse_vis, delta_vis, key_acc, value_acc)

    final = lax.fori_loop(
        0, cycle, backward_step, (queries, out_grad, zero_field, lse, delta, zero_field, zero_field)
    )
    query_acc, key_acc, value_acc = (final[2], final[5], final[6])
    return (
        attended,
        query_acc.astype(jnp.bfloat16),
        key_acc.astype(jnp.bfloat16),
        value_acc.astype(jnp.bfloat16),
    )


def solution(mesh):
    in_specs = (
        P(("image", "head"), None, "token"),
        P(("image", "head"), None, "token"),
        P(("image", "head"), None, "token"),
        P(("image", "head"), None, "token"),
        P(),
        P(),
    )
    out_specs = (
        P(("image", "head"), None, "token"),
        P(("image", "head"), None, "token"),
        P(("image", "head"), None, "token"),
        P(("image", "head"), None, "token"),
    )
    return jax.shard_map(body, mesh=mesh, in_specs=in_specs, out_specs=out_specs, check_vma=False)
```

profile of v0, /device:TPU:0, one launch (start us, length us, event | category | flops | bytes accessed | tf_op | source)
XLA Modules:
  0.0 305.7 jit_solution(5576349334511306710)
XLA Ops:
  2.6 1.3 dynamic_slice.36
  4.6 133.8 %while.48 = (s32[]{:T(128)}, bf16[4,80,512]{2,1,0:T(8,128)(2,1)S(1)}, f32[4,80,512]{2,1,0:T(8,128)S(1)}, f32[4,512]{1,0:T(4,128)S(1)}, f32[4,512]{1,0:T(4,128)S(...) while((s32[]{:T(128)}, ...), condition=%wide.region_5.6_spmd, body=%wide.region_0.5_spmd.sunk | while | flops 347418688 | bytes 22291100 | solution.py:85
  4.7 1.2 dynamic_slice.39
  6.0 2.0 fusion.63
  8.6 5.1 %conditional.4 = (f32[4,80,512]{2,1,0:T(8,128)S(1)}, f32[4,512]{1,0:T(4,128)}, f32[4,512]{1,0:T(4,128)S(1)}) conditional(s32[]{:T(128)} %convert_element_type.103, (f32[4,80,512]{2,1,0:T(8,128)S(1)}, f32[4,512]{1,0:T(4,128)S(1)}, f32[4,512]{1,0:T(4,128)S(1)}) %tuple.92, (pred[]{:T(512)}, bf16[4,80,512]{2,1,0:T(8,128)(2,1)S(1)}, ...), branch_computations={%region_1.1_spmd, %region_2.0_spmd} | conditional | flops 347418624 | bytes 16310327 | solution.py:75
  8.6 1.8 fusion
  13.7 3.1 %collective-permute-start.1 = (f32[4,80,512]{2,1,0:T(8,128)S(1)}, f32[4,80,512]{2,1,0:T(8,128)S(1)}, u32[]{:S(2)}, u32[]{:S(2)}) collective-permute-start(f32[4,80,512]{2,1,0:T(8,128)S(1)} %get-tuple-element.873), channel_id=1, source_target_pairs={{0,8},{8,16},{16,24},{24,0},{1,9},{9,17},{17,25},{25,1},{2,10},{10... | collective-permute-start | bytes 1966088 | tf_op jit(solution)/shard_map/while/body/eval_jaxpr/ppermute | solution.py:12
  16.8 1.6 collective-permute-start
  18.4 1.6 collective-permute-start.3
  20.0 20.8 %collective-permute-done.3 = f32[4,512]{1,0:T(4,128)S(1)} collective-permute-done((f32[4,512]{1,0:T(4,128)S(1)}, f32[4,512]{1,0:T(4,128)S(1)}, u32[]{:S(2)}, u32[]{:S(2)}) %collective-permute-start.3) | collective-permute-done | bytes 8224 | tf_op jit(solution)/shard_map/while/body/eval_jaxpr/ppermute | solution.py:12
  42.2 2.0 fusion.63
  45.5 4.3 %collective-permute-start.1 = (f32[4,80,512]{2,1,0:T(8,128)S(1)}, f32[4,80,512]{2,1,0:T(8,128)S(1)}, u32[]{:S(2)}, u32[]{:S(2)}) collective-permute-start(f32[4,80,512]{2,1,0:T(8,128)S(1)} %get-tuple-element.873), channel_id=1, source_target_pairs={{0,8},{8,16},{16,24},{24,0},{1,9},{9,17},{17,25},{25,1},{2,10},{10... | collective-permute-start | bytes 1966088 | tf_op jit(solution)/shard_map/while/body/eval_jaxpr/ppermute | solution.py:12
  49.8 1.6 collective-permute-start
  51.4 1.6 collective-permute-start.3
  53.0 19.9 %collective-permute-done.3 = f32[4,512]{1,0:T(4,128)S(1)} collective-permute-done((f32[4,512]{1,0:T(4,128)S(1)}, f32[4,512]{1,0:T(4,128)S(1)}, u32[]{:S(2)}, u32[]{:S(2)}) %collective-permute-start.3) | collective-permute-done | bytes 8224 | tf_op jit(solution)/shard_map/while/body/eval_jaxpr/ppermute | solution.py:12
  74.3 2.0 fusion.63
  77.0 5.1 %conditional.4 = (f32[4,80,512]{2,1,0:T(8,128)S(1)}, f32[4,512]{1,0:T(4,128)}, f32[4,512]{1,0:T(4,128)S(1)}) conditional(s32[]{:T(128)} %convert_element_type.103, (f32[4,80,512]{2,1,0:T(8,128)S(1)}, f32[4,512]{1,0:T(4,128)S(1)}, f32[4,512]{1,0:T(4,128)S(1)}) %tuple.92, (pred[]{:T(512)}, bf16[4,80,512]{2,1,0:T(8,128)(2,1)S(1)}, ...), branch_computations={%region_1.1_spmd, %region_2.0_spmd} | conditional | flops 347418624 | bytes 16310327 | solution.py:75
  77.0 1.8 fusion
  82.2 1.3 collective-permute-start
  83.4 1.6 collective-permute-start.3
  85.0 2.1 collective-permute-start.2
  87.1 19.0 %collective-permute-done.3 = f32[4,512]{1,0:T(4,128)S(1)} collective-permute-done((f32[4,512]{1,0:T(4,128)S(1)}, f32[4,512]{1,0:T(4,128)S(1)}, u32[]{:S(2)}, u32[]{:S(2)}) %collective-permute-start.3) | collective-permute-done | bytes 8224 | tf_op jit(solution)/shard_map/while/body/eval_jaxpr/ppermute | solution.py:12
  107.5 2.0 fusion.63
  110.2 5.1 %conditional.4 = (f32[4,80,512]{2,1,0:T(8,128)S(1)}, f32[4,512]{1,0:T(4,128)}, f32[4,512]{1,0:T(4,128)S(1)}) conditional(s32[]{:T(128)} %convert_element_type.103, (f32[4,80,512]{2,1,0:T(8,128)S(1)}, f32[4,512]{1,0:T(4,128)S(1)}, f32[4,512]{1,0:T(4,128)S(1)}) %tuple.92, (pred[]{:T(512)}, bf16[4,80,512]{2,1,0:T(8,128)(2,1)S(1)}, ...), branch_computations={%region_1.1_spmd, %region_2.0_spmd} | conditional | flops 347418624 | bytes 16310327 | solution.py:75
  110.2 1.8 fusion
  116.1 4.2 %collective-permute-start.2 = (f32[4,512]{1,0:T(4,128)}, f32[4,512]{1,0:T(4,128)S(1)}, u32[]{:S(2)}, u32[]{:S(2)}) collective-permute-start(f32[4,512]{1,0:T(4,128)} %get-tuple-element.874), channel_id=1, source_target_pairs={{0,8},{8,16},{16,24},{24,0},{1,9},{9,17},{17,25},{25,1},{2,10},{10... | collective-permute-start | bytes 24584 | tf_op jit(solution)/shard_map/while/body/eval_jaxpr/ppermute | solution.py:12
  120.3 18.1 %collective-permute-done.3 = f32[4,512]{1,0:T(4,128)S(1)} collective-permute-done((f32[4,512]{1,0:T(4,128)S(1)}, f32[4,512]{1,0:T(4,128)S(1)}, u32[]{:S(2)}, u32[]{:S(2)}) %collective-permute-start.3) | collective-permute-done | bytes 8224 | tf_op jit(solution)/shard_map/while/body/eval_jaxpr/ppermute | solution.py:12
  140.4 161.9 %while.49 = (s32[]{:T(128)}, bf16[4,80,512]{2,1,0:T(8,128)(2,1)S(1)}, bf16[4,80,512]{2,1,0:T(8,128)(2,1)S(1)}, f32[4,80,512]{2,1,0:T(8,128)S(1)}, f32[4,512]{1,0...) while((s32[]{:T(128)}, ...), condition=%wide.region_10.11_spmd, body=%wide.region_7.10_spmd.sunk | while | flops 850886720 | bytes 35709716 | solution.py:113
  141.2 1.3 dynamic_slice.40
  142.5 2.0 fusion.66
  145.1 8.8 %conditional.5 = ((f32[4,80,512]{2,1,0:T(8,128)S(1)}, f32[4,80,512]{2,1,0:T(8,128)S(1)}, f32[4,80,512]{2,1,0:T(8,128)})) conditional(s32[]{:T(128)} %convert_element_type.104, (f32[4,80,512]{2,1,0:T(8,128)S(1)}, f32[4,80,512]{2,1,0:T(8,128)S(1)}, f32[4,80,512]{2,1,0:T(8,128)}) %tuple.95, (pred[]{:T(512)}, bf16[4,80,512]{2,1,0:T(8,128)(2,1)S(1)}, ...), branch_computations={%region_8.8_spmd, %region_9.9_spmd} | conditional | flops 850886656 | bytes 27746392 | solution.py:106
  145.1 1.8 fusion.40
  146.9 2.6 multiply_convert_fusion
  150.8 3.1 %fusion.23 = f32[4,80,512]{2,1,0:T(8,128)} fusion(f32[4,80,512]{2,1,0:T(8,128)} %get-tuple-element.634, bf16[4,80,512]{2,1,0:T(8,128)(2,1)} %get-tuple-element.630, f32[4,512,512]{2,1,0:T(8,128)S(1)} %fusion.40, f32[4,512]{1,0:T(4,128)S(1)} %get-tuple-element.629, pred[]{:T(512)} %get-tuple-element.670), kind=kOutput, calls=%fused_computation.24 | convolution fusion | flops 172130304 | bytes 5840897 | tf_op jit(solution)/shard_map/while/body/eval_jaxpr/cond/branch_1_fun/hij,hdi->hdj/dot_general | solution.py:51
  154.6 4.3 %collective-permute-start.7 = (f32[4,512]{1,0:T(4,128)S(1)}, f32[4,512]{1,0:T(4,128)S(1)}, u32[]{:S(2)}, u32[]{:S(2)}) collective-permute-start(f32[4,512]{1,0:T(4,128)S(1)} %copy.55), channel_id=1, source_target_pairs={{0,8},{8,16},{16,24},{24,0},{1,9},{9,17},{17,25},{25,1},{2,10},{10... | collective-permute-start | bytes 24584 | tf_op jit(solution)/shard_map/while/body/eval_jaxpr/ppermute | solution.py:12
  158.9 14.5 %collective-permute-done.6 = f32[4,80,512]{2,1,0:T(8,128)S(1)} collective-permute-done((f32[4,80,512]{2,1,0:T(8,128)S(1)}, f32[4,80,512]{2,1,0:T(8,128)S(1)}, u32[]{:S(2)}, u32[]{:S(2)}) %collective-permute-start.6) | collective-permute-done | bytes 655392 | tf_op jit(solution)/shard_map/while/body/eval_jaxpr/ppermute | solution.py:12
  173.4 9.6 %collective-permute-done.7 = f32[4,512]{1,0:T(4,128)S(1)} collective-permute-done((f32[4,512]{1,0:T(4,128)S(1)}, f32[4,512]{1,0:T(4,128)S(1)}, u32[]{:S(2)}, u32[]{:S(2)}) %collective-permute-start.7) | collective-permute-done | bytes 8224 | tf_op jit(solution)/shard_map/while/body/eval_jaxpr/ppermute | solution.py:12
  183.9 1.3 dynamic_slice.40
  185.2 2.0 fusion.66
  187.8 7.3 %collective-permute-start.6 = (f32[4,80,512]{2,1,0:T(8,128)S(1)}, f32[4,80,512]{2,1,0:T(8,128)S(1)}, u32[]{:S(2)}, u32[]{:S(2)}) collective-permute-start(f32[4,80,512]{2,1,0:T(8,128)S(1)} %get-tuple-element.890), channel_id=1, source_target_pairs={{0,8},{8,16},{16,24},{24,0},{1,9},{9,17},{17,25},{25,1},{2,10},{10... | collective-permute-start | bytes 1966088 | tf_op jit(solution)/shard_map/while/body/eval_jaxpr/ppermute | solution.py:12
  195.1 2.2 collective-permute-start.5
  197.3 2.7 collective-permute-start.8
  200.1 11.8 %collective-permute-done.6 = f32[4,80,512]{2,1,0:T(8,128)S(1)} collective-permute-done((f32[4,80,512]{2,1,0:T(8,128)S(1)}, f32[4,80,512]{2,1,0:T(8,128)S(1)}, u32[]{:S(2)}, u32[]{:S(2)}) %collective-permute-start.6) | collective-permute-done | bytes 655392 | tf_op jit(solution)/shard_map/while/body/eval_jaxpr/ppermute | solution.py:12
  211.9 9.0 %collective-permute-done.7 = f32[4,512]{1,0:T(4,128)S(1)} collective-permute-done((f32[4,512]{1,0:T(4,128)S(1)}, f32[4,512]{1,0:T(4,128)S(1)}, u32[]{:S(2)}, u32[]{:S(2)}) %collective-permute-start.7) | collective-permute-done | bytes 8224 | tf_op jit(solution)/shard_map/while/body/eval_jaxpr/ppermute | solution.py:12
  221.7 1.3 dynamic_slice.40
  223.0 2.0 fusion.66
  225.6 8.8 %conditional.5 = ((f32[4,80,512]{2,1,0:T(8,128)S(1)}, f32[4,80,512]{2,1,0:T(8,128)S(1)}, f32[4,80,512]{2,1,0:T(8,128)})) conditional(s32[]{:T(128)} %convert_element_type.104, (f32[4,80,512]{2,1,0:T(8,128)S(1)}, f32[4,80,512]{2,1,0:T(8,128)S(1)}, f32[4,80,512]{2,1,0:T(8,128)}) %tuple.95, (pred[]{:T(512)}, bf16[4,80,512]{2,1,0:T(8,128)(2,1)S(1)}, ...), branch_computations={%region_8.8_spmd, %region_9.9_spmd} | conditional | flops 850886656 | bytes 27746392 | solution.py:106
  225.6 1.8 fusion.40
  227.4 2.6 multiply_convert_fusion
  231.3 3.1 %fusion.23 = f32[4,80,512]{2,1,0:T(8,128)} fusion(f32[4,80,512]{2,1,0:T(8,128)} %get-tuple-element.634, bf16[4,80,512]{2,1,0:T(8,128)(2,1)} %get-tuple-element.630, f32[4,512,512]{2,1,0:T(8,128)S(1)} %fusion.40, f32[4,512]{1,0:T(4,128)S(1)} %get-tuple-element.629, pred[]{:T(512)} %get-tuple-element.670), kind=kOutput, calls=%fused_computation.24 | convolution fusion | flops 172130304 | bytes 5840897 | tf_op jit(solution)/shard_map/while/body/eval_jaxpr/cond/branch_1_fun/hij,hdi->hdj/dot_general | solution.py:51
  235.7 1.6 collective-permute-start.5
  237.3 2.1 collective-permute-start.7
  240.3 13.6 %collective-permute-done.6 = f32[4,80,512]{2,1,0:T(8,128)S(1)} collective-permute-done((f32[4,80,512]{2,1,0:T(8,128)S(1)}, f32[4,80,512]{2,1,0:T(8,128)S(1)}, u32[]{:S(2)}, u32[]{:S(2)}) %collective-permute-start.6) | collective-permute-done | bytes 655392 | tf_op jit(solution)/shard_map/while/body/eval_jaxpr/ppermute | solution.py:12
  253.9 8.0 %collective-permute-done.7 = f32[4,512]{1,0:T(4,128)S(1)} collective-permute-done((f32[4,512]{1,0:T(4,128)S(1)}, f32[4,512]{1,0:T(4,128)S(1)}, u32[]{:S(2)}, u32[]{:S(2)}) %collective-permute-start.7) | collective-permute-done | bytes 8224 | tf_op jit(solution)/shard_map/while/body/eval_jaxpr/ppermute | solution.py:12
  262.8 1.3 dynamic_slice.40
  264.1 2.0 fusion.66
  266.8 8.8 %conditional.5 = ((f32[4,80,512]{2,1,0:T(8,128)S(1)}, f32[4,80,512]{2,1,0:T(8,128)S(1)}, f32[4,80,512]{2,1,0:T(8,128)})) conditional(s32[]{:T(128)} %convert_element_type.104, (f32[4,80,512]{2,1,0:T(8,128)S(1)}, f32[4,80,512]{2,1,0:T(8,128)S(1)}, f32[4,80,512]{2,1,0:T(8,128)}) %tuple.95, (pred[]{:T(512)}, bf16[4,80,512]{2,1,0:T(8,128)(2,1)S(1)}, ...), branch_computations={%region_8.8_spmd, %region_9.9_spmd} | conditional | flops 850886656 | bytes 27746392 | solution.py:106
  266.8 1.8 fusion.40
  268.6 2.6 multiply_convert_fusion
  272.5 3.1 %fusion.23 = f32[4,80,512]{2,1,0:T(8,128)} fusion(f32[4,80,512]{2,1,0:T(8,128)} %get-tuple-element.634, bf16[4,80,512]{2,1,0:T(8,128)(2,1)} %get-tuple-element.630, f32[4,512,512]{2,1,0:T(8,128)S(1)} %fusion.40, f32[4,512]{1,0:T(4,128)S(1)} %get-tuple-element.629, pred[]{:T(512)} %get-tuple-element.670), kind=kOutput, calls=%fused_computation.24 | convolution fusion | flops 172130304 | bytes 5840897 | tf_op jit(solution)/shard_map/while/body/eval_jaxpr/cond/branch_1_fun/hij,hdi->hdj/dot_general | solution.py:51
  276.3 4.2 %collective-permute-start.7 = (f32[4,512]{1,0:T(4,128)S(1)}, f32[4,512]{1,0:T(4,128)S(1)}, u32[]{:S(2)}, u32[]{:S(2)}) collective-permute-start(f32[4,512]{1,0:T(4,128)S(1)} %copy.55), channel_id=1, source_target_pairs={{0,8},{8,16},{16,24},{24,0},{1,9},{9,17},{17,25},{25,1},{2,10},{10... | collective-permute-start | bytes 24584 | tf_op jit(solution)/shard_map/while/body/eval_jaxpr/ppermute | solution.py:12
  280.5 14.5 %collective-permute-done.6 = f32[4,80,512]{2,1,0:T(8,128)S(1)} collective-permute-done((f32[4,80,512]{2,1,0:T(8,128)S(1)}, f32[4,80,512]{2,1,0:T(8,128)S(1)}, u32[]{:S(2)}, u32[]{:S(2)}) %collective-permute-start.6) | collective-permute-done | bytes 655392 | tf_op jit(solution)/shard_map/while/body/eval_jaxpr/ppermute | solution.py:12
  295.1 7.1 %collective-permute-done.7 = f32[4,512]{1,0:T(4,128)S(1)} collective-permute-done((f32[4,512]{1,0:T(4,128)S(1)}, f32[4,512]{1,0:T(4,128)S(1)}, u32[]{:S(2)}, u32[]{:S(2)}) %collective-permute-start.7) | collective-permute-done | bytes 8224 | tf_op jit(solution)/shard_map/while/body/eval_jaxpr/ppermute | solution.py:12
  303.8 1.9 convert_element_type.83
  (131 shorter events, 33.8 us)
Async XLA Ops:
  8.6 4.0 %copy-start.1 = (bf16[4,80,512]{2,1,0:T(8,128)(2,1)S(1)}, bf16[4,80,512]{2,1,0:T(8,128)(2,1)}, u32[]{:S(2)}) copy-start(bf16[4,80,512]{2,1,0:T(8,128)(2,1)} %get-tuple-element.608) | copy-start | bytes 983044 | tf_op jit(solution)/shard_map/while/body/eval_jaxpr/cond
  13.7 27.1 %collective-permute-start.1 = (f32[4,80,512]{2,1,0:T(8,128)S(1)}, f32[4,80,512]{2,1,0:T(8,128)S(1)}, u32[]{:S(2)}, u32[]{:S(2)}) collective-permute-start(f32[4,80,512]{2,1,0:T(8,128)S(1)} %get-tuple-element.873), channel_id=1, source_target_pairs={{0,8},{8,16},{16,24},{24,0},{1,9},{9,17},{17,25},{25,1},{2,10},{10... | collective-permute-start | bytes 1966088 | tf_op jit(solution)/shard_map/while/body/eval_jaxpr/ppermute | solution.py:12
  16.8 24.1 %collective-permute-start = (bf16[4,80,512]{2,1,0:T(8,128)(2,1)S(1)}, bf16[4,80,512]{2,1,0:T(8,128)(2,1)S(1)}, u32[]{:S(2)}, u32[]{:S(2)}) collective-permute-start(bf16[4,80,512]{2,1,0:T(8,128)(2,1)S(1)} %copy.34), channel_id=1, source_target_pairs={{0,8},{8,16},{16,24},{24,0},{1,9},{9,17},{17,25},{25,1},{2,10},{10... | collective-permute-start | bytes 983048 | tf_op jit(solution)/shard_map/while/body/eval_jaxpr/ppermute | solution.py:12
  18.4 22.5 %collective-permute-start.3 = (f32[4,512]{1,0:T(4,128)S(1)}, f32[4,512]{1,0:T(4,128)S(1)}, u32[]{:S(2)}, u32[]{:S(2)}) collective-permute-start(f32[4,512]{1,0:T(4,128)S(1)} %get-tuple-element.875), channel_id=1, source_target_pairs={{0,8},{8,16},{16,24},{24,0},{1,9},{9,17},{17,25},{25,1},{2,10},{10... | collective-permute-start | bytes 24584 | tf_op jit(solution)/shard_map/while/body/eval_jaxpr/ppermute | solution.py:12
  20.0 21.0 %collective-permute-start.2 = (f32[4,512]{1,0:T(4,128)}, f32[4,512]{1,0:T(4,128)S(1)}, u32[]{:S(2)}, u32[]{:S(2)}) collective-permute-start(f32[4,512]{1,0:T(4,128)} %get-tuple-element.874), channel_id=1, source_target_pairs={{0,8},{8,16},{16,24},{24,0},{1,9},{9,17},{17,25},{25,1},{2,10},{10... | collective-permute-start | bytes 24584 | tf_op jit(solution)/shard_map/while/body/eval_jaxpr/ppermute | solution.py:12
  45.5 27.4 %collective-permute-start.1 = (f32[4,80,512]{2,1,0:T(8,128)S(1)}, f32[4,80,512]{2,1,0:T(8,128)S(1)}, u32[]{:S(2)}, u32[]{:S(2)}) collective-permute-start(f32[4,80,512]{2,1,0:T(8,128)S(1)} %get-tuple-element.873), channel_id=1, source_target_pairs={{0,8},{8,16},{16,24},{24,0},{1,9},{9,17},{17,25},{25,1},{2,10},{10... | collective-permute-start | bytes 1966088 | tf_op jit(solution)/shard_map/while/body/eval_jaxpr/ppermute | solution.py:12
  49.8 23.2 %collective-permute-start = (bf16[4,80,512]{2,1,0:T(8,128)(2,1)S(1)}, bf16[4,80,512]{2,1,0:T(8,128)(2,1)S(1)}, u32[]{:S(2)}, u32[]{:S(2)}) collective-permute-start(bf16[4,80,512]{2,1,0:T(8,128)(2,1)S(1)} %copy.34), channel_id=1, source_target_pairs={{0,8},{8,16},{16,24},{24,0},{1,9},{9,17},{17,25},{25,1},{2,10},{10... | collective-permute-start | bytes 983048 | tf_op jit(solution)/shard_map/while/body/eval_jaxpr/ppermute | solution.py:12
  51.4 21.6 %collective-permute-start.3 = (f32[4,512]{1,0:T(4,128)S(1)}, f32[4,512]{1,0:T(4,128)S(1)}, u32[]{:S(2)}, u32[]{:S(2)}) collective-permute-start(f32[4,512]{1,0:T(4,128)S(1)} %get-tuple-element.875), channel_id=1, source_target_pairs={{0,8},{8,16},{16,24},{24,0},{1,9},{9,17},{17,25},{25,1},{2,10},{10... | collective-permute-start | bytes 24584 | tf_op jit(solution)/shard_map/while/body/eval_jaxpr/ppermute | solution.py:12
  52.9 20.1 %collective-permute-start.2 = (f32[4,512]{1,0:T(4,128)}, f32[4,512]{1,0:T(4,128)S(1)}, u32[]{:S(2)}, u32[]{:S(2)}) collective-permute-start(f32[4,512]{1,0:T(4,128)} %get-tuple-element.874), channel_id=1, source_target_pairs={{0,8},{8,16},{16,24},{24,0},{1,9},{9,17},{17,25},{25,1},{2,10},{10... | collective-permute-start | bytes 24584 | tf_op jit(solution)/shard_map/while/body/eval_jaxpr/ppermute | solution.py:12
  77.0 4.0 %copy-start.1 = (bf16[4,80,512]{2,1,0:T(8,128)(2,1)S(1)}, bf16[4,80,512]{2,1,0:T(8,128)(2,1)}, u32[]{:S(2)}) copy-start(bf16[4,80,512]{2,1,0:T(8,128)(2,1)} %get-tuple-element.608) | copy-start | bytes 983044 | tf_op jit(solution)/shard_map/while/body/eval_jaxpr/cond
  82.1 24.0 %collective-permute-start.1 = (f32[4,80,512]{2,1,0:T(8,128)S(1)}, f32[4,80,512]{2,1,0:T(8,128)S(1)}, u32[]{:S(2)}, u32[]{:S(2)}) collective-permute-start(f32[4,80,512]{2,1,0:T(8,128)S(1)} %get-tuple-element.873), channel_id=1, source_target_pairs={{0,8},{8,16},{16,24},{24,0},{1,9},{9,17},{17,25},{25,1},{2,10},{10... | collective-permute-start | bytes 1966088 | tf_op jit(solution)/shard_map/while/body/eval_jaxpr/ppermute | solution.py:12
  82.2 24.1 %collective-permute-start = (bf16[4,80,512]{2,1,0:T(8,128)(2,1)S(1)}, bf16[4,80,512]{2,1,0:T(8,128)(2,1)S(1)}, u32[]{:S(2)}, u32[]{:S(2)}) collective-permute-start(bf16[4,80,512]{2,1,0:T(8,128)(2,1)S(1)} %copy.34), channel_id=1, source_target_pairs={{0,8},{8,16},{16,24},{24,0},{1,9},{9,17},{17,25},{25,1},{2,10},{10... | collective-permute-start | bytes 983048 | tf_op jit(solution)/shard_map/while/body/eval_jaxpr/ppermute | solution.py:12
  83.4 22.7 %collective-permute-start.3 = (f32[4,512]{1,0:T(4,128)S(1)}, f32[4,512]{1,0:T(4,128)S(1)}, u32[]{:S(2)}, u32[]{:S(2)}) collective-permute-start(f32[4,512]{1,0:T(4,128)S(1)} %get-tuple-element.875), channel_id=1, source_target_pairs={{0,8},{8,16},{16,24},{24,0},{1,9},{9,17},{17,25},{25,1},{2,10},{10... | collective-permute-start | bytes 24584 | tf_op jit(solution)/shard_map/while/body/eval_jaxpr/ppermute | solution.py:12
  85.0 21.2 %collective-permute-start.2 = (f32[4,512]{1,0:T(4,128)}, f32[4,512]{1,0:T(4,128)S(1)}, u32[]{:S(2)}, u32[]{:S(2)}) collective-permute-start(f32[4,512]{1,0:T(4,128)} %get-tuple-element.874), channel_id=1, source_target_pairs={{0,8},{8,16},{16,24},{24,0},{1,9},{9,17},{17,25},{25,1},{2,10},{10... | collective-permute-start | bytes 24584 | tf_op jit(solution)/shard_map/while/body/eval_jaxpr/ppermute | solution.py:12
  110.2 4.0 %copy-start.1 = (bf16[4,80,512]{2,1,0:T(8,128)(2,1)S(1)}, bf16[4,80,512]{2,1,0:T(8,128)(2,1)}, u32[]{:S(2)}) copy-start(bf16[4,80,512]{2,1,0:T(8,128)(2,1)} %get-tuple-element.608) | copy-start | bytes 983044 | tf_op jit(solution)/shard_map/while/body/eval_jaxpr/cond
  115.3 23.1 %collective-permute-start.1 = (f32[4,80,512]{2,1,0:T(8,128)S(1)}, f32[4,80,512]{2,1,0:T(8,128)S(1)}, u32[]{:S(2)}, u32[]{:S(2)}) collective-permute-start(f32[4,80,512]{2,1,0:T(8,128)S(1)} %get-tuple-element.873), channel_id=1, source_target_pairs={{0,8},{8,16},{16,24},{24,0},{1,9},{9,17},{17,25},{25,1},{2,10},{10... | collective-permute-start | bytes 1966088 | tf_op jit(solution)/shard_map/while/body/eval_jaxpr/ppermute | solution.py:12
  115.4 23.1 %collective-permute-start = (bf16[4,80,512]{2,1,0:T(8,128)(2,1)S(1)}, bf16[4,80,512]{2,1,0:T(8,128)(2,1)S(1)}, u32[]{:S(2)}, u32[]{:S(2)}) collective-permute-start(bf16[4,80,512]{2,1,0:T(8,128)(2,1)S(1)} %copy.34), channel_id=1, source_target_pairs={{0,8},{8,16},{16,24},{24,0},{1,9},{9,17},{17,25},{25,1},{2,10},{10... | collective-permute-start | bytes 983048 | tf_op jit(solution)/shard_map/while/body/eval_jaxpr/ppermute | solution.py:12
  115.4 23.0 %collective-permute-start.3 = (f32[4,512]{1,0:T(4,128)S(1)}, f32[4,512]{1,0:T(4,128)S(1)}, u32[]{:S(2)}, u32[]{:S(2)}) collective-permute-start(f32[4,512]{1,0:T(4,128)S(1)} %get-tuple-element.875), channel_id=1, source_target_pairs={{0,8},{8,16},{16,24},{24,0},{1,9},{9,17},{17,25},{25,1},{2,10},{10... | collective-permute-start | bytes 24584 | tf_op jit(solution)/shard_map/while/body/eval_jaxpr/ppermute | solution.py:12
  116.1 22.3 %collective-permute-start.2 = (f32[4,512]{1,0:T(4,128)}, f32[4,512]{1,0:T(4,128)S(1)}, u32[]{:S(2)}, u32[]{:S(2)}) collective-permute-start(f32[4,512]{1,0:T(4,128)} %get-tuple-element.874), channel_id=1, source_target_pairs={{0,8},{8,16},{16,24},{24,0},{1,9},{9,17},{17,25},{25,1},{2,10},{10... | collective-permute-start | bytes 24584 | tf_op jit(solution)/shard_map/while/body/eval_jaxpr/ppermute | solution.py:12
  145.1 1.8 copy-start.2
  146.9 3.1 %copy-start = (bf16[4,80,512]{2,1,0:T(8,128)(2,1)S(1)}, bf16[4,80,512]{2,1,0:T(8,128)(2,1)}, u32[]{:S(2)}) copy-start(bf16[4,80,512]{2,1,0:T(8,128)(2,1)} %get-tuple-element.628) | copy-start | bytes 983044 | tf_op jit(solution)/shard_map/while/body/eval_jaxpr/cond
  153.9 19.5 %collective-permute-start.6 = (f32[4,80,512]{2,1,0:T(8,128)S(1)}, f32[4,80,512]{2,1,0:T(8,128)S(1)}, u32[]{:S(2)}, u32[]{:S(2)}) collective-permute-start(f32[4,80,512]{2,1,0:T(8,128)S(1)} %get-tuple-element.890), channel_id=1, source_target_pairs={{0,8},{8,16},{16,24},{24,0},{1,9},{9,17},{17,25},{25,1},{2,10},{10... | collective-permute-start | bytes 1966088 | tf_op jit(solution)/shard_map/while/body/eval_jaxpr/ppermute | solution.py:12
  153.9 29.2 %collective-permute-start.4 = (bf16[4,80,512]{2,1,0:T(8,128)(2,1)S(1)}, bf16[4,80,512]{2,1,0:T(8,128)(2,1)S(1)}, u32[]{:S(2)}, u32[]{:S(2)}) collective-permute-start(bf16[4,80,512]{2,1,0:T(8,128)(2,1)S(1)} %copy.52), channel_id=1, source_target_pairs={{0,8},{8,16},{16,24},{24,0},{1,9},{9,17},{17,25},{25,1},{2,10},{10... | collective-permute-start | bytes 983048 | tf_op jit(solution)/shard_map/while/body/eval_jaxpr/ppermute | solution.py:12
  153.9 29.2 %collective-permute-start.5 = (bf16[4,80,512]{2,1,0:T(8,128)(2,1)}, bf16[4,80,512]{2,1,0:T(8,128)(2,1)S(1)}, u32[]{:S(2)}, u32[]{:S(2)}) collective-permute-start(bf16[4,80,512]{2,1,0:T(8,128)(2,1)} %copy.53), channel_id=1, source_target_pairs={{0,8},{8,16},{16,24},{24,0},{1,9},{9,17},{17,25},{25,1},{2,10},{10... | collective-permute-start | bytes 983048 | tf_op jit(solution)/shard_map/while/body/eval_jaxpr/ppermute | solution.py:12
  154.6 28.4 %collective-permute-start.7 = (f32[4,512]{1,0:T(4,128)S(1)}, f32[4,512]{1,0:T(4,128)S(1)}, u32[]{:S(2)}, u32[]{:S(2)}) collective-permute-start(f32[4,512]{1,0:T(4,128)S(1)} %copy.55), channel_id=1, source_target_pairs={{0,8},{8,16},{16,24},{24,0},{1,9},{9,17},{17,25},{25,1},{2,10},{10... | collective-permute-start | bytes 24584 | tf_op jit(solution)/shard_map/while/body/eval_jaxpr/ppermute | solution.py:12
  158.9 24.3 %collective-permute-start.8 = (f32[4,512]{1,0:T(4,128)S(1)}, f32[4,512]{1,0:T(4,128)S(1)}, u32[]{:S(2)}, u32[]{:S(2)}) collective-permute-start(f32[4,512]{1,0:T(4,128)S(1)} %copy.56), channel_id=1, source_target_pairs={{0,8},{8,16},{16,24},{24,0},{1,9},{9,17},{17,25},{25,1},{2,10},{10... | collective-permute-start | bytes 24584 | tf_op jit(solution)/shard_map/while/body/eval_jaxpr/ppermute | solution.py:12
  187.8 24.0 %collective-permute-start.6 = (f32[4,80,512]{2,1,0:T(8,128)S(1)}, f32[4,80,512]{2,1,0:T(8,128)S(1)}, u32[]{:S(2)}, u32[]{:S(2)}) collective-permute-start(f32[4,80,512]{2,1,0:T(8,128)S(1)} %get-tuple-element.890), channel_id=1, source_target_pairs={{0,8},{8,16},{16,24},{24,0},{1,9},{9,17},{17,25},{25,1},{2,10},{10... | collective-permute-start | bytes 1966088 | tf_op jit(solution)/shard_map/while/body/eval_jaxpr/ppermute | solution.py:12
  195.1 25.8 %collective-permute-start.4 = (bf16[4,80,512]{2,1,0:T(8,128)(2,1)S(1)}, bf16[4,80,512]{2,1,0:T(8,128)(2,1)S(1)}, u32[]{:S(2)}, u32[]{:S(2)}) collective-permute-start(bf16[4,80,512]{2,1,0:T(8,128)(2,1)S(1)} %copy.52), channel_id=1, source_target_pairs={{0,8},{8,16},{16,24},{24,0},{1,9},{9,17},{17,25},{25,1},{2,10},{10... | collective-permute-start | bytes 983048 | tf_op jit(solution)/shard_map/while/body/eval_jaxpr/ppermute | solution.py:12
  195.1 25.8 %collective-permute-start.5 = (bf16[4,80,512]{2,1,0:T(8,128)(2,1)}, bf16[4,80,512]{2,1,0:T(8,128)(2,1)S(1)}, u32[]{:S(2)}, u32[]{:S(2)}) collective-permute-start(bf16[4,80,512]{2,1,0:T(8,128)(2,1)} %copy.53), channel_id=1, source_target_pairs={{0,8},{8,16},{16,24},{24,0},{1,9},{9,17},{17,25},{25,1},{2,10},{10... | collective-permute-start | bytes 983048 | tf_op jit(solution)/shard_map/while/body/eval_jaxpr/ppermute | solution.py:12
  197.3 23.5 %collective-permute-start.7 = (f32[4,512]{1,0:T(4,128)S(1)}, f32[4,512]{1,0:T(4,128)S(1)}, u32[]{:S(2)}, u32[]{:S(2)}) collective-permute-start(f32[4,512]{1,0:T(4,128)S(1)} %copy.55), channel_id=1, source_target_pairs={{0,8},{8,16},{16,24},{24,0},{1,9},{9,17},{17,25},{25,1},{2,10},{10... | collective-permute-start | bytes 24584 | tf_op jit(solution)/shard_map/while/body/eval_jaxpr/ppermute | solution.py:12
  197.3 23.6 %collective-permute-start.8 = (f32[4,512]{1,0:T(4,128)S(1)}, f32[4,512]{1,0:T(4,128)S(1)}, u32[]{:S(2)}, u32[]{:S(2)}) collective-permute-start(f32[4,512]{1,0:T(4,128)S(1)} %copy.56), channel_id=1, source_target_pairs={{0,8},{8,16},{16,24},{24,0},{1,9},{9,17},{17,25},{25,1},{2,10},{10... | collective-permute-start | bytes 24584 | tf_op jit(solution)/shard_map/while/body/eval_jaxpr/ppermute | solution.py:12
  225.6 1.8 copy-start.2
  227.4 3.1 %copy-start = (bf16[4,80,512]{2,1,0:T(8,128)(2,1)S(1)}, bf16[4,80,512]{2,1,0:T(8,128)(2,1)}, u32[]{:S(2)}) copy-start(bf16[4,80,512]{2,1,0:T(8,128)(2,1)} %get-tuple-element.628) | copy-start | bytes 983044 | tf_op jit(solution)/shard_map/while/body/eval_jaxpr/cond
  234.4 19.5 %collective-permute-start.6 = (f32[4,80,512]{2,1,0:T(8,128)S(1)}, f32[4,80,512]{2,1,0:T(8,128)S(1)}, u32[]{:S(2)}, u32[]{:S(2)}) collective-permute-start(f32[4,80,512]{2,1,0:T(8,128)S(1)} %get-tuple-element.890), channel_id=1, source_target_pairs={{0,8},{8,16},{16,24},{24,0},{1,9},{9,17},{17,25},{25,1},{2,10},{10... | collective-permute-start | bytes 1966088 | tf_op jit(solution)/shard_map/while/body/eval_jaxpr/ppermute | solution.py:12
  235.4 26.7 %collective-permute-start.4 = (bf16[4,80,512]{2,1,0:T(8,128)(2,1)S(1)}, bf16[4,80,512]{2,1,0:T(8,128)(2,1)S(1)}, u32[]{:S(2)}, u32[]{:S(2)}) collective-permute-start(bf16[4,80,512]{2,1,0:T(8,128)(2,1)S(1)} %copy.52), channel_id=1, source_target_pairs={{0,8},{8,16},{16,24},{24,0},{1,9},{9,17},{17,25},{25,1},{2,10},{10... | collective-permute-start | bytes 983048 | tf_op jit(solution)/shard_map/while/body/eval_jaxpr/ppermute | solution.py:12
  235.7 26.4 %collective-permute-start.5 = (bf16[4,80,512]{2,1,0:T(8,128)(2,1)}, bf16[4,80,512]{2,1,0:T(8,128)(2,1)S(1)}, u32[]{:S(2)}, u32[]{:S(2)}) collective-permute-start(bf16[4,80,512]{2,1,0:T(8,128)(2,1)} %copy.53), channel_id=1, source_target_pairs={{0,8},{8,16},{16,24},{24,0},{1,9},{9,17},{17,25},{25,1},{2,10},{10... | collective-permute-start | bytes 983048 | tf_op jit(solution)/shard_map/while/body/eval_jaxpr/ppermute | solution.py:12
  237.3 24.7 %collective-permute-start.7 = (f32[4,512]{1,0:T(4,128)S(1)}, f32[4,512]{1,0:T(4,128)S(1)}, u32[]{:S(2)}, u32[]{:S(2)}) collective-permute-start(f32[4,512]{1,0:T(4,128)S(1)} %copy.55), channel_id=1, source_target_pairs={{0,8},{8,16},{16,24},{24,0},{1,9},{9,17},{17,25},{25,1},{2,10},{10... | collective-permute-start | bytes 24584 | tf_op jit(solution)/shard_map/while/body/eval_jaxpr/ppermute | solution.py:12
  239.4 22.7 %collective-permute-start.8 = (f32[4,512]{1,0:T(4,128)S(1)}, f32[4,512]{1,0:T(4,128)S(1)}, u32[]{:S(2)}, u32[]{:S(2)}) collective-permute-start(f32[4,512]{1,0:T(4,128)S(1)} %copy.56), channel_id=1, source_target_pairs={{0,8},{8,16},{16,24},{24,0},{1,9},{9,17},{17,25},{25,1},{2,10},{10... | collective-permute-start | bytes 24584 | tf_op jit(solution)/shard_map/while/body/eval_jaxpr/ppermute | solution.py:12
  266.8 1.8 copy-start.2
  268.6 3.1 %copy-start = (bf16[4,80,512]{2,1,0:T(8,128)(2,1)S(1)}, bf16[4,80,512]{2,1,0:T(8,128)(2,1)}, u32[]{:S(2)}) copy-start(bf16[4,80,512]{2,1,0:T(8,128)(2,1)} %get-tuple-element.628) | copy-start | bytes 983044 | tf_op jit(solution)/shard_map/while/body/eval_jaxpr/cond
  275.5 19.5 %collective-permute-start.6 = (f32[4,80,512]{2,1,0:T(8,128)S(1)}, f32[4,80,512]{2,1,0:T(8,128)S(1)}, u32[]{:S(2)}, u32[]{:S(2)}) collective-permute-start(f32[4,80,512]{2,1,0:T(8,128)S(1)} %get-tuple-element.890), channel_id=1, source_target_pairs={{0,8},{8,16},{16,24},{24,0},{1,9},{9,17},{17,25},{25,1},{2,10},{10... | collective-permute-start | bytes 1966088 | tf_op jit(solution)/shard_map/while/body/eval_jaxpr/ppermute | solution.py:12
  275.5 26.7 %collective-permute-start.4 = (bf16[4,80,512]{2,1,0:T(8,128)(2,1)S(1)}, bf16[4,80,512]{2,1,0:T(8,128)(2,1)S(1)}, u32[]{:S(2)}, u32[]{:S(2)}) collective-permute-start(bf16[4,80,512]{2,1,0:T(8,128)(2,1)S(1)} %copy.52), channel_id=1, source_target_pairs={{0,8},{8,16},{16,24},{24,0},{1,9},{9,17},{17,25},{25,1},{2,10},{10... | collective-permute-start | bytes 983048 | tf_op jit(solution)/shard_map/while/body/eval_jaxpr/ppermute | solution.py:12
  275.6 26.7 %collective-permute-start.5 = (bf16[4,80,512]{2,1,0:T(8,128)(2,1)}, bf16[4,80,512]{2,1,0:T(8,128)(2,1)S(1)}, u32[]{:S(2)}, u32[]{:S(2)}) collective-permute-start(bf16[4,80,512]{2,1,0:T(8,128)(2,1)} %copy.53), channel_id=1, source_target_pairs={{0,8},{8,16},{16,24},{24,0},{1,9},{9,17},{17,25},{25,1},{2,10},{10... | collective-permute-start | bytes 983048 | tf_op jit(solution)/shard_map/while/body/eval_jaxpr/ppermute | solution.py:12
  276.3 25.8 %collective-permute-start.7 = (f32[4,512]{1,0:T(4,128)S(1)}, f32[4,512]{1,0:T(4,128)S(1)}, u32[]{:S(2)}, u32[]{:S(2)}) collective-permute-start(f32[4,512]{1,0:T(4,128)S(1)} %copy.55), channel_id=1, source_target_pairs={{0,8},{8,16},{16,24},{24,0},{1,9},{9,17},{17,25},{25,1},{2,10},{10... | collective-permute-start | bytes 24584 | tf_op jit(solution)/shard_map/while/body/eval_jaxpr/ppermute | solution.py:12
  280.5 21.8 %collective-permute-start.8 = (f32[4,512]{1,0:T(4,128)S(1)}, f32[4,512]{1,0:T(4,128)S(1)}, u32[]{:S(2)}, u32[]{:S(2)}) collective-permute-start(f32[4,512]{1,0:T(4,128)S(1)} %copy.56), channel_id=1, source_target_pairs={{0,8},{8,16},{16,24},{24,0},{1,9},{9,17},{17,25},{25,1},{2,10},{10... | collective-permute-start | bytes 24584 | tf_op jit(solution)/shard_map/while/body/eval_jaxpr/ppermute | solution.py:12
where the time goes:
time: 307 us; the launch traced here: 306 us
  waiting for transfers between devices  166 us (54%)
  starting transfers between devices  51.9 us (17%)
  matrix products  50.8 us (17%)
  local copies, waits for them, and re-layouts  18.6 us (6%)
  other arithmetic  11.4 us (4%)
  loops' own time  5.87 us (2%)
    ppermute x36, waiting for transfers between devices, from_behind(): return lax.ppermute(value, axis, pairs)  166 us
    ppermute x36, starting transfers between devices, from_behind(): return lax.ppermute(value, axis, pairs)  51.9 us
    dot_general x8, matrix products, block_pairs(): jnp.dot(query_hot, flags.astype(jnp.float32))  16 us
    dot_general x6, matrix products, masked_scores(): jnp.einsum('hdi,hdj->hij', query, key, preferred_element_type=jnp.float32)  10.7 us
    dynamic_slice x8, local copies, waits for them, and re-layouts, block_pairs(): query_ids = lax.dynamic_slice_in_dim(order, query_dev * per, per)  10.2 us
    dot_general x3, matrix products, backward_tile(): jnp.einsum('hij,hdi->hdj', prob.astype(jnp.bfloat16), grad, preferred_ele...  9.22 us
    dot_general x3, matrix products, backward_tile(): jnp.einsum('hdi,hdj->hij', grad, value, preferred_element_type=jnp.float32)  7.71 us
  transfers between devices with their start and end apart: 36, of which 16 were waited for; matrix products, arithmetic and copies ran while one was open for 0% of the time, Pallas kernels for 0%

commit v1 on v0

--- a/solution.py
+++ b/solution.py
@@ -1,6 +1,10 @@
+import functools
+
 import jax
 import jax.numpy as jnp
 from jax import lax
+from jax.experimental import pallas as pl
+from jax.experimental.pallas import tpu as pltpu
 from jax.sharding import PartitionSpec as P
 
 BLK = 512
@@ -58,7 +62,7 @@
     return (query_part, key_part, value_part)
 
 
-def body(queries, keys, values, out_grad, flags, order):
+def ring_body(queries, keys, values, out_grad, flags, order):
     cycle = lax.axis_size("token")
     me = lax.axis_index("token")
     heads, dim, toks = queries.shape
@@ -122,6 +126,221 @@
     )
 
 
+NT = (((1,), (1,)), ((), ()))
+LOG2E = 1.4426950408889634
+SUB = 256
+
+
+def dot(a, b):
+    return jnp.dot(a, b, preferred_element_type=jnp.float32)
+
+
+def dot_nt(a, b):
+    return lax.dot_general(a, b, NT, preferred_element_type=jnp.float32)
+
+
+def swap_kernel(
+    n, flags, order, q_in, k_in, v_in, g_in, o_out, dq_out, dk_out, dv_out,
+    qb, kb, vb, gb, kt, vt, score, prob, dk_acc, dv_acc, ob, dqb, dkb, dvb,
+    in_send, in_recv, out_send, out_recv,
+):
+    me = lax.axis_index("token")
+    dim, blk = qb.shape[1:]
+    scale = dim ** (-0.5)
+    expo = scale * LOG2E
+    ins = ((k_in, kb), (v_in, vb), (q_in, qb), (g_in, gb))
+    outs = ((ob, o_out), (dqb, dq_out), (dkb, dk_out), (dvb, dv_out))
+    offs = [n // 2] + [o for o in range(1, n) if o != n // 2]
+
+    def other(off):
+        return lax.rem(me + off, n)
+
+    def send_in(t, off):
+        src, dst = ins[t]
+        to = other(off)
+        return pltpu.make_async_remote_copy(
+            src_ref=src.at[to], dst_ref=dst.at[me], send_sem=in_send.at[t, off],
+            recv_sem=in_recv.at[t, me], device_id={"token": to},
+        )
+
+    def take_in(t, frm):
+        src, dst = ins[t]
+        return pltpu.make_async_remote_copy(
+            src_ref=src.at[me], dst_ref=dst.at[frm], send_sem=in_send.at[t, 0],
+            recv_sem=in_recv.at[t, frm], device_id={"token": frm},
+        )
+
+    def own_in(t):
+        src, dst = ins[t]
+        return pltpu.make_async_copy(src.at[me], dst.at[me], in_recv.at[t, me])
+
+    def send_out(t, to):
+        src, dst = outs[t]
+        return pltpu.make_async_remote_copy(
+            src_ref=src.at[to], dst_ref=dst.at[me], send_sem=out_send.at[t, to],
+            recv_sem=out_recv.at[t, me], device_id={"token": to},
+        )
+
+    def take_out(t, frm):
+        src, dst = outs[t]
+        return pltpu.make_async_remote_copy(
+            src_ref=src.at[me], dst_ref=dst.at[frm], send_sem=out_send.at[t, me],
+            recv_sem=out_recv.at[t, frm], device_id={"token": frm},
+        )
+
+    def own_out(t):
+        src, dst = outs[t]
+        return pltpu.make_async_copy(src.at[me], dst.at[me], out_recv.at[t, me])
+
+    for t in range(4):
+        own_in(t).start()
+    barrier = pltpu.get_barrier_semaphore()
+    for off in range(1, n):
+        pl.semaphore_signal(barrier, inc=1, device_id={"token": other(off)})
+    pl.semaphore_wait(barrier, n - 1)
+
+    for t in range(2):
+        for off in offs:
+            send_in(t, off).start()
+    dk_acc[...] = jnp.zeros_like(dk_acc)
+    dv_acc[...] = jnp.zeros_like(dv_acc)
+    for t in range(4):
+        own_in(t).wait()
+    for off in offs:
+        send_in(0, off).wait_send()
+    for off in offs:
+        for t in (2, 3):
+            send_in(t, off).start()
+    for off in offs:
+        take_in(0, other(off)).wait_recv()
+    for j in range(n):
+        kt[j] = kb[j].astype(jnp.float32).T.astype(jnp.bfloat16)
+    for off in offs:
+        take_in(1, other(off)).wait_recv()
+    for j in range(n):
+        vt[j] = vb[j].astype(jnp.float32).T.astype(jnp.bfloat16)
+
+    parts = blk // SUB
+
+    def step(i, carry):
+        turn, sub = i // parts, lax.rem(i, parts)
+        off = jnp.where(turn == 0, 0, jnp.where(turn == 1, n // 2, jnp.where(turn <= n // 2, turn - 1, turn)))
+        row = other(off)
+        cols = pl.ds(pl.multiple_of(sub * SUB, SUB), SUB)
+
+        @pl.when(jnp.logical_and(turn > 0, sub == 0))
+        def _():
+            take_in(2, row).wait_recv()
+            take_in(3, row).wait_recv()
+
+        label = order[row]
+        bias = [jnp.where(flags[label, order[j]] != 0, 0.0, -jnp.inf) for j in range(n)]
+        q = qb[row, :, cols]
+        g = gb[row, :, cols]
+        top = None
+        for j in range(n):
+            s = dot(kt[j], q)
+            score[j] = s
+            m = jnp.max(s, axis=0, keepdims=True) + bias[j]
+            top = m if top is None else jnp.maximum(top, m)
+        top = top * expo
+        total = jnp.zeros_like(top)
+        o = jnp.zeros((dim, SUB), jnp.float32)
+        for j in range(n):
+            p = jnp.exp2(score[j] * expo - (top - bias[j]))
+            total += jnp.sum(p, axis=0, keepdims=True)
+            low = p.astype(jnp.bfloat16)
+            prob[j] = low
+            o += dot(vb[j], low)
+        inv = 1.0 / total
+        att = (o * inv).astype(jnp.bfloat16)
+        ob[row, :, cols] = att
+        gf = g.astype(jnp.float32)
+        delta = jnp.sum(gf * att.astype(jnp.float32), axis=0, keepdims=True)
+        gs = (gf * inv).astype(jnp.bfloat16)
+        qs = (q.astype(jnp.float32) * (inv * scale)).astype(jnp.bfloat16)
+        dq = jnp.zeros((dim, SUB), jnp.float32)
+        for j in range(n):
+            low = prob[j]
+            dp = dot(vt[j], g)
+            ds = (low.astype(jnp.float32) * (dp - delta)).astype(jnp.bfloat16)
+            dv_acc[j] += dot_nt(gs, low)
+            dk_acc[j] += dot_nt(qs, ds)
+            dq += dot(kb[j], ds)
+        dqb[row, :, cols] = (dq * (inv * scale)).astype(jnp.bfloat16)
+
+        @pl.when(jnp.logical_and(turn == 0, sub == parts - 1))
+        def _():
+            for t in range(2):
+                own_out(t).start()
+
+        @pl.when(jnp.logical_and(turn > 0, sub == parts - 1))
+        def _():
+            for t in range(2):
+                send_out(t, row).start()
+
+        return carry
+
+    lax.fori_loop(0, n * parts, step, 0)
+
+    dkb[...] = dk_acc[...].astype(jnp.bfloat16)
+    dvb[...] = dv_acc[...].astype(jnp.bfloat16)
+    for off in offs:
+        for t in (2, 3):
+            send_out(t, other(off)).start()
+    for t in (2, 3):
+        own_out(t).start()
+    for t in range(1, 4):
+        for off in offs:
+            send_in(t, off).wait_send()
+    for t in range(4):
+        own_out(t).wait()
+        for off in offs:
+            send_out(t, other(off)).wait_send()
+            take_out(t, other(off)).wait_recv()
+
+
+def swap_body(queries, keys, values, out_grad, flags, order):
+    n = lax.axis_size("token")
+    heads, dim, blk = queries.shape
+    low = pltpu.VMEM((n, dim, blk), jnp.bfloat16)
+    wide = pltpu.VMEM((n, dim, blk), jnp.float32)
+    turned = pltpu.VMEM((n, blk, dim), jnp.bfloat16)
+    anywhere = pl.BlockSpec(memory_space=pl.ANY)
+    smem = pl.BlockSpec(memory_space=pltpu.SMEM)
+    sems = pltpu.SemaphoreType.DMA((4, n))
+    toks = n * blk
+    return tuple(
+        pl.pallas_call(
+            functools.partial(swap_kernel, n),
+            out_shape=[jax.ShapeDtypeStruct(queries.shape, jnp.bfloat16)] * 4,
+            in_specs=[smem, smem] + [anywhere] * 4,
+            out_specs=[anywhere] * 4,
+            scratch_shapes=[low] * 4
+            + [turned] * 2
+            + [pltpu.VMEM((n, blk, SUB), jnp.float32), pltpu.VMEM((n, blk, SUB), jnp.bfloat16)]
+            + [wide] * 2
+            + [low] * 4
+            + [sems] * 4,
+            compiler_params=pltpu.CompilerParams(
+                collective_id=0, has_side_effects=True, vmem_limit_bytes=40 * 1024 * 1024
+            ),
+            cost_estimate=pl.CostEstimate(
+                flops=12 * dim * toks * toks, bytes_accessed=16 * heads * dim * blk,
+                transcendentals=toks * toks,
+            ),
+        )(flags, order, queries, keys, values, out_grad)
+    )
+
+
+def body(queries, keys, values, out_grad, flags, order):
+    n = lax.axis_size("token")
+    heads, _, toks = queries.shape
+    if n > 1 and n % 2 == 0 and heads == n and toks == BLK:
+        return swap_body(queries, keys, values, out_grad, flags, order)
+    return ring_body(queries, keys, values, out_grad, flags, order)
+
+
 def solution(mesh):
     in_specs = (
         P(("image", "head"), None, "token"),

time: 307 us -> 73.9 us (0.24)
  waiting for transfers between devices: 166 us -> 0 us
  Pallas kernels: 0 us -> 64.7 us
  starting transfers between devices: 51.9 us -> 0 us
  matrix products: 50.8 us -> 0 us
  other arithmetic: 11.4 us -> 0 us
  local copies, waits for them, and re-layouts: 18.6 us -> 8.12 us
  loops' own time: 5.87 us -> 0 us
    ppermute x36 -> x0, waiting for transfers between devices: 166 us -> none  [from_behind(): return lax.ppermute(value, axis, pairs)]
    pallas_call x0 -> x1, Pallas kernels: none -> 64.7 us  [swap_body(): pl.pallas_call(functools.partial(swap_kernel, n), out_shape=[jax.ShapeDty...]
    ppermute x36 -> x0, starting transfers between devices: 51.9 us -> none  [from_behind(): return lax.ppermute(value, axis, pairs)]
    dot_general x29 -> x0, matrix products: 50.8 us -> none  [the longest x8 16 us: block_pairs(): jnp.dot(query_hot, flags.astype(jnp.float32))]
    dynamic_slice x9 -> x0, local copies, waits for them, and re-layouts: 11.4 us -> none  [the longest x8 10.2 us: block_pairs(): query_ids = lax.dynamic_slice_in_dim(order, query_dev * per, per)]
    unnamed x3 -> x16, local copies, waits for them, and re-layouts: 1.97 us -> 8.12 us
    another operation x10 -> x0, loops' own time: 5.87 us -> none  [the longest x1 2.85 us: body(): lax.fori_loop(0, cycle, forward_step, (queries, zero_field, start_max, ze...]
    convert_element_type x4 -> x0, other arithmetic: 4.07 us -> none  [the longest x1 1.85 us: body(): value_acc.astype(jnp.bfloat16)]
  transfers between devices with their start and end apart: 36 -> 0, of which waited for: 16 -> 0; matrix products, arithmetic and copies ran while one was open for 0% -> 0% of each run, Pallas kernels for 0% -> 0%
where the time goes in v1:
time: 73.9 us; the launch traced here: 73.4 us
  Pallas kernels  64.7 us (88%)
  local copies, waits for them, and re-layouts  8.12 us (11%)
    pallas_call x1, Pallas kernels, swap_body(): pl.pallas_call(functools.partial(swap_kernel, n), out_shape=[jax.ShapeDty...  64.7 us
    unnamed x16, local copies, waits for them, and re-layouts  8.12 us

profile of v1, /device:TPU:0, one launch (start us, length us, event | category | flops | bytes accessed | tf_op | source)
XLA Modules:
  0.0 73.4 jit_solution(17032237956577353478)
XLA Ops:
  0.6 0.0 copy-start
  0.6 1.0 %copy-done = bf16[4,80,512]{2,1,0:T(8,128)(2,1)S(1)} copy-done((bf16[4,80,512]{2,1,0:T(8,128)(2,1)S(1)}, bf16[4,80,512]{2,1,0:T(8,128)(2,1)}, u32[]{:S(2)}) %copy-start) | copy-done | bytes 327704
  1.6 0.0 copy-start.1
  1.6 1.0 %copy-done.1 = bf16[4,80,512]{2,1,0:T(8,128)(2,1)S(1)} copy-done((bf16[4,80,512]{2,1,0:T(8,128)(2,1)S(1)}, bf16[4,80,512]{2,1,0:T(8,128)(2,1)}, u32[]{:S(2)}) %copy-start.1) | copy-done | bytes 327704
  2.6 0.0 copy-start.2
  2.6 1.0 %copy-done.2 = bf16[4,80,512]{2,1,0:T(8,128)(2,1)S(1)} copy-done((bf16[4,80,512]{2,1,0:T(8,128)(2,1)S(1)}, bf16[4,80,512]{2,1,0:T(8,128)(2,1)}, u32[]{:S(2)}) %copy-start.2) | copy-done | bytes 327704
  3.6 0.0 copy-start.3
  3.6 1.0 %copy-done.3 = bf16[4,80,512]{2,1,0:T(8,128)(2,1)S(1)} copy-done((bf16[4,80,512]{2,1,0:T(8,128)(2,1)S(1)}, bf16[4,80,512]{2,1,0:T(8,128)(2,1)}, u32[]{:S(2)}) %copy-start.3) | copy-done | bytes 327704
  4.5 0.0 copy-start.4
  4.5 0.7 copy-done.4
  5.2 0.0 copy-start.5
  5.2 0.7 copy-done.5
  5.9 64.7 %shard_map.93 = (bf16[4,80,512]{2,1,0:T(8,128)(2,1)S(1)}, bf16[4,80,512]{2,1,0:T(8,128)(2,1)S(1)}, bf16[4,80,512]{2,1,0:T(8,128)(2,1)S(1)}, bf16[4,80,512]{2,1,0:T(8,128)(2,1)S(1)}) custom-call(s32[4,4]{1,0:T(4,128)S(1)} %copy-done.4, s32[4]{0:T(128)S(1)} %copy-done.5, bf16[4,80,512]{2,1,0:T(8,128)(2,1)S(1)} %copy-done, bf16[4,80,512]{2,1,0:T(8,128)(2,1)S(1)} %copy-done.1, ...), custom_call_target="tpu_custom_call" | custom-call | flops 4026531840 | bytes 2621440 | tf_op jit(solution)/shard_map/pallas_call | solution.py:314
  70.5 0.7 copy.14
  71.3 0.7 copy.15
  72.0 0.7 copy.16
  72.7 0.7 copy.17
Async XLA Ops:
  0.6 1.0 %copy-start = (bf16[4,80,512]{2,1,0:T(8,128)(2,1)S(1)}, bf16[4,80,512]{2,1,0:T(8,128)(2,1)}, u32[]{:S(2)}) copy-start(bf16[4,80,512]{2,1,0:T(8,128)(2,1)} %q_in.1) | copy-start | bytes 983044
  1.6 1.0 %copy-start.1 = (bf16[4,80,512]{2,1,0:T(8,128)(2,1)S(1)}, bf16[4,80,512]{2,1,0:T(8,128)(2,1)}, u32[]{:S(2)}) copy-start(bf16[4,80,512]{2,1,0:T(8,128)(2,1)} %k_in.1) | copy-start | bytes 983044
  2.6 1.0 %copy-start.2 = (bf16[4,80,512]{2,1,0:T(8,128)(2,1)S(1)}, bf16[4,80,512]{2,1,0:T(8,128)(2,1)}, u32[]{:S(2)}) copy-start(bf16[4,80,512]{2,1,0:T(8,128)(2,1)} %v_in.1) | copy-start | bytes 983044
  3.6 1.0 %copy-start.3 = (bf16[4,80,512]{2,1,0:T(8,128)(2,1)S(1)}, bf16[4,80,512]{2,1,0:T(8,128)(2,1)}, u32[]{:S(2)}) copy-start(bf16[4,80,512]{2,1,0:T(8,128)(2,1)} %g_in.1) | copy-start | bytes 983044
  4.5 0.7 copy-start.4
  5.2 0.7 copy-start.5

commit v2 on v1

--- a/solution.py
+++ b/solution.py
@@ -300,6 +300,30 @@
             take_out(t, other(off)).wait_recv()
 
 
+def place_kernel(*refs):
+    ins, outs, sems = refs[:4], refs[4:8], refs[8]
+    copies = [pltpu.make_async_copy(ins[t], outs[t], sems.at[t]) for t in range(4)]
+    for copy in copies:
+        copy.start()
+    for copy in copies:
+        copy.wait()
+
+
+def place(results):
+    anywhere = pl.BlockSpec(memory_space=pl.ANY)
+    size = sum(r.size * 4 for r in results)
+    return tuple(
+        pl.pallas_call(
+            place_kernel,
+            out_shape=[jax.ShapeDtypeStruct(r.shape, r.dtype) for r in results],
+            in_specs=[pl.BlockSpec(memory_space=pltpu.VMEM)] * 4,
+            out_specs=[pl.BlockSpec(memory_space=pltpu.HBM)] * 4,
+            scratch_shapes=[pltpu.SemaphoreType.DMA((4,))],
+            cost_estimate=pl.CostEstimate(flops=0, bytes_accessed=size, transcendentals=0),
+        )(*results)
+    )
+
+
 def swap_body(queries, keys, values, out_grad, flags, order):
     n = lax.axis_size("token")
     heads, dim, blk = queries.shape
@@ -310,7 +334,7 @@
     smem = pl.BlockSpec(memory_space=pltpu.SMEM)
     sems = pltpu.SemaphoreType.DMA((4, n))
     toks = n * blk
-    return tuple(
+    return place(
         pl.pallas_call(
             functools.partial(swap_kernel, n),
             out_shape=[jax.ShapeDtypeStruct(queries.shape, jnp.bfloat16)] * 4,
@@ -323,7 +347,7 @@
             + [low] * 4
             + [sems] * 4,
             compiler_params=pltpu.CompilerParams(
-                collective_id=0, has_side_effects=True, vmem_limit_bytes=40 * 1024 * 1024
+                collective_id=0, has_side_effects=True, vmem_limit_bytes=60 * 1024 * 1024
             ),
             cost_estimate=pl.CostEstimate(
                 flops=12 * dim * toks * toks, bytes_accessed=16 * heads * dim * blk,

time: 73.9 us -> 68.1 us (0.922)
  local copies, waits for them, and re-layouts: 8.12 us -> 0 us
  Pallas kernels: 64.7 us -> 67.1 us
    unnamed x16 -> x0, local copies, waits for them, and re-layouts: 8.12 us -> none
    pallas_call x0 -> x1, Pallas kernels: none -> 2.35 us  [place(): pl.pallas_call(place_kernel, out_shape=[jax.ShapeDtypeStruct(r.shape, r.d...]
where the time goes in v2:
time: 68.1 us; the launch traced here: 67.7 us
  Pallas kernels  67.1 us (99%)
    pallas_call x1, Pallas kernels, swap_body(): pl.pallas_call(functools.partial(swap_kernel, n), out_shape=[jax.ShapeDty...  64.7 us
    pallas_call x1, Pallas kernels, place(): pl.pallas_call(place_kernel, out_shape=[jax.ShapeDtypeStruct(r.shape, r.d...  2.35 us

profile of v2, /device:TPU:0, one launch (start us, length us, event | category | flops | bytes accessed | tf_op | source)
XLA Modules:
  0.0 67.7 jit_solution(1194045716989743277)
XLA Ops:
  0.6 64.7 %shard_map.93 = (bf16[4,80,512]{2,1,0:T(8,128)(2,1)}, bf16[4,80,512]{2,1,0:T(8,128)(2,1)}, bf16[4,80,512]{2,1,0:T(8,128)(2,1)}, bf16[4,80,512]{2,1,0:T(8,128)(2,1)}) custom-call(s32[4,4]{1,0:T(4,128)} %flags.1, s32[4]{0:T(128)} %order.1, bf16[4,80,512]{2,1,0:T(8,128)(2,1)} %q_in.1, bf16[4,80,512]{2,1,0:T(8,128)(2,1)} %k_in.1, bf16[4,80,512]{2,1,0:T(8,128)(2,1)} %v_in.1, ...), custom_call_target="tpu_custom_call" | custom-call | flops 4026531840 | bytes 2621440 | tf_op jit(solution)/shard_map/pallas_call | solution.py:338
  65.3 2.4 %shard_map.94 = (bf16[4,80,512]{2,1,0:T(8,128)(2,1)}, bf16[4,80,512]{2,1,0:T(8,128)(2,1)}, bf16[4,80,512]{2,1,0:T(8,128)(2,1)}, bf16[4,80,512]{2,1,0:T(8,128)(2,1)}) custom-call(bf16[4,80,512]{2,1,0:T(8,128)(2,1)} %get-tuple-element.8.refs_0_, bf16[4,80,512]{2,1,0:T(8,128)(2,1)} %get-tuple-element.9.refs_1_, bf16[4,80,512]{2,1,0:T(8,128)(2,1)} %get-tuple-element.10.refs_2_, ...), custom_call_target="tpu_custom_call" | custom-call | bytes 2621440 | tf_op jit(solution)/shard_map/pallas_call | solution.py:316

commit v3 on v2

--- a/solution.py
+++ b/solution.py
@@ -126,7 +126,6 @@
     )
 
 
-NT = (((1,), (1,)), ((), ()))
 LOG2E = 1.4426950408889634
 SUB = 256
 
@@ -135,8 +134,12 @@
     return jnp.dot(a, b, preferred_element_type=jnp.float32)
 
 
-def dot_nt(a, b):
-    return lax.dot_general(a, b, NT, preferred_element_type=jnp.float32)
+def crossed(a, b, n):
+    out, w = 0, 1
+    while w < n:
+        out = out + w * lax.rem(lax.div(a, jnp.int32(w)) + lax.div(jnp.int32(b), jnp.int32(w)), jnp.int32(2))
+        w *= 2
+    return out
 
 
 def swap_kernel(
@@ -150,10 +153,11 @@
     expo = scale * LOG2E
     ins = ((k_in, kb), (v_in, vb), (q_in, qb), (g_in, gb))
     outs = ((ob, o_out), (dqb, dq_out), (dkb, dk_out), (dvb, dv_out))
-    offs = [n // 2] + [o for o in range(1, n) if o != n // 2]
+    offs = list(range(1, n))
+    far = offs[n // 2 - 1:] + offs[:n // 2 - 1]
 
     def other(off):
-        return lax.rem(me + off, n)
+        return crossed(me, off, n)
 
     def send_in(t, off):
         src, dst = ins[t]
@@ -200,7 +204,7 @@
     pl.semaphore_wait(barrier, n - 1)
 
     for t in range(2):
-        for off in offs:
+        for off in far:
             send_in(t, off).start()
     dk_acc[...] = jnp.zeros_like(dk_acc)
     dv_acc[...] = jnp.zeros_like(dv_acc)
@@ -223,9 +227,8 @@
     parts = blk // SUB
 
     def step(i, carry):
-        turn, sub = i // parts, lax.rem(i, parts)
-        off = jnp.where(turn == 0, 0, jnp.where(turn == 1, n // 2, jnp.where(turn <= n // 2, turn - 1, turn)))
-        row = other(off)
+        turn, sub = lax.div(i, parts), lax.rem(i, parts)
+        row = other(turn)
         cols = pl.ds(pl.multiple_of(sub * SUB, SUB), SUB)
 
         @pl.when(jnp.logical_and(turn > 0, sub == 0))
@@ -257,15 +260,15 @@
         ob[row, :, cols] = att
         gf = g.astype(jnp.float32)
         delta = jnp.sum(gf * att.astype(jnp.float32), axis=0, keepdims=True)
-        gs = (gf * inv).astype(jnp.bfloat16)
-        qs = (q.astype(jnp.float32) * (inv * scale)).astype(jnp.bfloat16)
+        gs = (gf * inv).T.astype(jnp.bfloat16)
+        qs = (q.astype(jnp.float32) * (inv * scale)).T.astype(jnp.bfloat16)
         dq = jnp.zeros((dim, SUB), jnp.float32)
         for j in range(n):
             low = prob[j]
             dp = dot(vt[j], g)
             ds = (low.astype(jnp.float32) * (dp - delta)).astype(jnp.bfloat16)
-            dv_acc[j] += dot_nt(gs, low)
-            dk_acc[j] += dot_nt(qs, ds)
+            dv_acc[j] += dot(low, gs)
+            dk_acc[j] += dot(ds, qs)
             dq += dot(kb[j], ds)
         dqb[row, :, cols] = (dq * (inv * scale)).astype(jnp.bfloat16)
 
@@ -283,9 +286,10 @@
 
     lax.fori_loop(0, n * parts, step, 0)
 
-    dkb[...] = dk_acc[...].astype(jnp.bfloat16)
-    dvb[...] = dv_acc[...].astype(jnp.bfloat16)
-    for off in offs:
+    for j in range(n):
+        dkb[j] = dk_acc[j].T.astype(jnp.bfloat16)
+        dvb[j] = dv_acc[j].T.astype(jnp.bfloat16)
+    for off in far:
         for t in (2, 3):
             send_out(t, other(off)).start()
     for t in (2, 3):
@@ -328,7 +332,7 @@
     n = lax.axis_size("token")
     heads, dim, blk = queries.shape
     low = pltpu.VMEM((n, dim, blk), jnp.bfloat16)
-    wide = pltpu.VMEM((n, dim, blk), jnp.float32)
+    wide = pltpu.VMEM((n, blk, dim), jnp.float32)
     turned = pltpu.VMEM((n, blk, dim), jnp.bfloat16)
     anywhere = pl.BlockSpec(memory_space=pl.ANY)
     smem = pl.BlockSpec(memory_space=pltpu.SMEM)
@@ -360,7 +364,7 @@
 def body(queries, keys, values, out_grad, flags, order):
     n = lax.axis_size("token")
     heads, _, toks = queries.shape
-    if n > 1 and n % 2 == 0 and heads == n and toks == BLK:
+    if n > 1 and n & (n - 1) == 0 and heads == n and toks == BLK:
         return swap_body(queries, keys, values, out_grad, flags, order)
     return ring_body(queries, keys, values, out_grad, flags, order)
 

time: 68.1 us -> 66.5 us (0.977)
  Pallas kernels: 67.1 us -> 65 us
    pallas_call x1, Pallas kernels: 64.7 us -> 62.6 us  [swap_body(): pl.pallas_call(functools.partial(swap_kernel, n), out_shape=[jax.ShapeDty...]
where the time goes in v3:
time: 66.5 us; the launch traced here: 65.6 us
  Pallas kernels  65 us (98%)
    pallas_call x1, Pallas kernels, swap_body(): pl.pallas_call(functools.partial(swap_kernel, n), out_shape=[jax.ShapeDty...  62.6 us
    pallas_call x1, Pallas kernels, place(): pl.pallas_call(place_kernel, out_shape=[jax.ShapeDtypeStruct(r.shape, r.d...  2.35 us

profile of v3, /device:TPU:0, one launch (start us, length us, event | category | flops | bytes accessed | tf_op | source)
XLA Modules:
  0.0 65.6 jit_solution(7628331467902936129)
XLA Ops:
  0.6 62.6 %shard_map.93 = (bf16[4,80,512]{2,1,0:T(8,128)(2,1)}, bf16[4,80,512]{2,1,0:T(8,128)(2,1)}, bf16[4,80,512]{2,1,0:T(8,128)(2,1)}, bf16[4,80,512]{2,1,0:T(8,128)(2,1)}) custom-call(s32[4,4]{1,0:T(4,128)} %flags.1, s32[4]{0:T(128)} %order.1, bf16[4,80,512]{2,1,0:T(8,128)(2,1)} %q_in.1, bf16[4,80,512]{2,1,0:T(8,128)(2,1)} %k_in.1, bf16[4,80,512]{2,1,0:T(8,128)(2,1)} %v_in.1, ...), custom_call_target="tpu_custom_call" | custom-call | flops 4026531840 | bytes 2621440 | tf_op jit(solution)/shard_map/pallas_call | solution.py:342
  63.3 2.4 %shard_map.94 = (bf16[4,80,512]{2,1,0:T(8,128)(2,1)}, bf16[4,80,512]{2,1,0:T(8,128)(2,1)}, bf16[4,80,512]{2,1,0:T(8,128)(2,1)}, bf16[4,80,512]{2,1,0:T(8,128)(2,1)}) custom-call(bf16[4,80,512]{2,1,0:T(8,128)(2,1)} %get-tuple-element.8.refs_0_, bf16[4,80,512]{2,1,0:T(8,128)(2,1)} %get-tuple-element.9.refs_1_, bf16[4,80,512]{2,1,0:T(8,128)(2,1)} %get-tuple-element.10.refs_2_, ...), custom_call_target="tpu_custom_call" | custom-call | bytes 2621440 | tf_op jit(solution)/shard_map/pallas_call | solution.py:320

commit v4 on v3

--- a/solution.py
+++ b/solution.py
@@ -127,7 +127,7 @@
 
 
 LOG2E = 1.4426950408889634
-SUB = 256
+SUB = 512
 
 
 def dot(a, b):
@@ -143,9 +143,9 @@
 
 
 def swap_kernel(
-    n, flags, order, q_in, k_in, v_in, g_in, o_out, dq_out, dk_out, dv_out,
+    n, flags_in, order_in, q_in, k_in, v_in, g_in, o_out, dq_out, dk_out, dv_out,
     qb, kb, vb, gb, kt, vt, score, prob, dk_acc, dv_acc, ob, dqb, dkb, dvb,
-    in_send, in_recv, out_send, out_recv,
+    in_send, in_recv, out_send, out_recv, flags, order, table_sem,
 ):
     me = lax.axis_index("token")
     dim, blk = qb.shape[1:]
@@ -196,11 +196,17 @@
         src, dst = outs[t]
         return pltpu.make_async_copy(src.at[me], dst.at[me], out_recv.at[t, me])
 
-    for t in range(4):
-        own_in(t).start()
     barrier = pltpu.get_barrier_semaphore()
     for off in range(1, n):
         pl.semaphore_signal(barrier, inc=1, device_id={"token": other(off)})
+    tables = [
+        pltpu.make_async_copy(flags_in, flags, table_sem.at[0]),
+        pltpu.make_async_copy(order_in, order, table_sem.at[1]),
+    ]
+    for copy in tables:
+        copy.start()
+    for t in range(4):
+        own_in(t).start()
     pl.semaphore_wait(barrier, n - 1)
 
     for t in range(2):
@@ -208,6 +214,8 @@
             send_in(t, off).start()
     dk_acc[...] = jnp.zeros_like(dk_acc)
     dv_acc[...] = jnp.zeros_like(dv_acc)
+    for copy in tables:
+        copy.wait()
     for t in range(4):
         own_in(t).wait()
     for off in offs:
@@ -324,7 +332,7 @@
             out_specs=[pl.BlockSpec(memory_space=pltpu.HBM)] * 4,
             scratch_shapes=[pltpu.SemaphoreType.DMA((4,))],
             cost_estimate=pl.CostEstimate(flops=0, bytes_accessed=size, transcendentals=0),
-        )(*results)
+        )(*[pltpu.with_memory_space_constraint(r, pltpu.VMEM) for r in results])
     )
 
 
@@ -335,21 +343,22 @@
     wide = pltpu.VMEM((n, blk, dim), jnp.float32)
     turned = pltpu.VMEM((n, blk, dim), jnp.bfloat16)
     anywhere = pl.BlockSpec(memory_space=pl.ANY)
-    smem = pl.BlockSpec(memory_space=pltpu.SMEM)
     sems = pltpu.SemaphoreType.DMA((4, n))
     toks = n * blk
     return place(
         pl.pallas_call(
             functools.partial(swap_kernel, n),
-            out_shape=[jax.ShapeDtypeStruct(queries.shape, jnp.bfloat16)] * 4,
-            in_specs=[smem, smem] + [anywhere] * 4,
-            out_specs=[anywhere] * 4,
+            out_shape=[pltpu.VMEM(queries.shape, jnp.bfloat16)] * 4,
+            in_specs=[anywhere] * 6,
+            out_specs=[pl.BlockSpec(memory_space=pltpu.VMEM)] * 4,
             scratch_shapes=[low] * 4
             + [turned] * 2
             + [pltpu.VMEM((n, blk, SUB), jnp.float32), pltpu.VMEM((n, blk, SUB), jnp.bfloat16)]
             + [wide] * 2
             + [low] * 4
-            + [sems] * 4,
+            + [sems] * 4
+            + [pltpu.SMEM(flags.shape, jnp.int32), pltpu.SMEM(order.shape, jnp.int32)]
+            + [pltpu.SemaphoreType.DMA((2,))],
             compiler_params=pltpu.CompilerParams(
                 collective_id=0, has_side_effects=True, vmem_limit_bytes=60 * 1024 * 1024
             ),

time: 66.5 us -> 63.7 us (0.958)
  Pallas kernels: 65 us -> 62.7 us
    pallas_call x1, Pallas kernels: 2.35 us -> 1.09 us  [place(): pl.pallas_call(place_kernel, out_shape=[jax.ShapeDtypeStruct(r.shape, r.d...]
    pallas_call x1, Pallas kernels: 62.6 us -> 61.6 us  [swap_body(): pl.pallas_call(functools.partial(swap_kernel, n), out_shape=[pltpu.VMEM(q...]
where the time goes in v4:
time: 63.7 us; the launch traced here: 63.4 us
  Pallas kernels  62.7 us (98%)
  between operations  0.64 us (1%)
    pallas_call x1, Pallas kernels, swap_body(): pl.pallas_call(functools.partial(swap_kernel, n), out_shape=[pltpu.VMEM(q...  61.6 us

profile of v4, /device:TPU:0, one launch (start us, length us, event | category | flops | bytes accessed | tf_op | source)
XLA Modules:
  0.0 63.4 jit_solution(16916462345937684350)
XLA Ops:
  0.6 61.6 %shard_map.93 = (bf16[4,80,512]{2,1,0:T(8,128)(2,1)S(1)}, bf16[4,80,512]{2,1,0:T(8,128)(2,1)S(1)}, bf16[4,80,512]{2,1,0:T(8,128)(2,1)S(1)}, bf16[4,80,512]{2,1,0:T(8,128)(2,1)S(1)}) custom-call(s32[4,4]{1,0:T(4,128)} %flags_in.1, s32[4]{0:T(128)} %order_in.1, bf16[4,80,512]{2,1,0:T(8,128)(2,1)} %q_in.1, bf16[4,80,512]{2,1,0:T(8,128)(2,1)} %k_in.1, ...), custom_call_target="tpu_custom_call" | custom-call | flops 4026531840 | bytes 2621440 | tf_op jit(solution)/shard_map/pallas_call | solution.py:349
  62.3 1.1 %shard_map.94 = (bf16[4,80,512]{2,1,0:T(8,128)(2,1)}, bf16[4,80,512]{2,1,0:T(8,128)(2,1)}, bf16[4,80,512]{2,1,0:T(8,128)(2,1)}, bf16[4,80,512]{2,1,0:T(8,128)(2,1)}) custom-call(bf16[4,80,512]{2,1,0:T(8,128)(2,1)S(1)} %get-tuple-element.8.refs_0_, bf16[4,80,512]{2,1,0:T(8,128)(2,1)S(1)} %get-tuple-element.9.refs_1_, ...), custom_call_target="tpu_custom_call" | custom-call | bytes 2621440 | tf_op jit(solution)/shard_map/pallas_call | solution.py:328

commit v5 on v4

--- a/solution.py
+++ b/solution.py
@@ -227,10 +227,6 @@
         take_in(0, other(off)).wait_recv()
     for j in range(n):
         kt[j] = kb[j].astype(jnp.float32).T.astype(jnp.bfloat16)
-    for off in offs:
-        take_in(1, other(off)).wait_recv()
-    for j in range(n):
-        vt[j] = vb[j].astype(jnp.float32).T.astype(jnp.bfloat16)
 
     parts = blk // SUB
 
@@ -254,6 +250,14 @@
             score[j] = s
             m = jnp.max(s, axis=0, keepdims=True) + bias[j]
             top = m if top is None else jnp.maximum(top, m)
+
+        @pl.when(i == 0)
+        def _():
+            for near in offs:
+                take_in(1, other(near)).wait_recv()
+            for j in range(n):
+                vt[j] = vb[j].astype(jnp.float32).T.astype(jnp.bfloat16)
+
         top = top * expo
         total = jnp.zeros_like(top)
         o = jnp.zeros((dim, SUB), jnp.float32)

time: 63.7 us -> 62.7 us (0.984); the launches traced: 63.4 us -> 61.6 us
  Pallas kernels: 62.7 us -> 61 us
    pallas_call x1, Pallas kernels: 61.6 us -> 59.9 us  [swap_body(): pl.pallas_call(functools.partial(swap_kernel, n), out_shape=[pltpu.VMEM(q...]
where the time goes in v5:
time: 62.7 us; the launch traced here: 61.6 us
  Pallas kernels  61 us (97%)
  between operations  0.64 us (1%)
    pallas_call x1, Pallas kernels, swap_body(): pl.pallas_call(functools.partial(swap_kernel, n), out_shape=[pltpu.VMEM(q...  59.9 us

profile of v5, /device:TPU:0, one launch (start us, length us, event | category | flops | bytes accessed | tf_op | source)
XLA Modules:
  0.0 61.6 jit_solution(13728217559523381050)
XLA Ops:
  0.6 59.9 %shard_map.93 = (bf16[4,80,512]{2,1,0:T(8,128)(2,1)S(1)}, bf16[4,80,512]{2,1,0:T(8,128)(2,1)S(1)}, bf16[4,80,512]{2,1,0:T(8,128)(2,1)S(1)}, bf16[4,80,512]{2,1,0:T(8,128)(2,1)S(1)}) custom-call(s32[4,4]{1,0:T(4,128)} %flags_in.1, s32[4]{0:T(128)} %order_in.1, bf16[4,80,512]{2,1,0:T(8,128)(2,1)} %q_in.1, bf16[4,80,512]{2,1,0:T(8,128)(2,1)} %k_in.1, ...), custom_call_target="tpu_custom_call" | custom-call | flops 4026531840 | bytes 2621440 | tf_op jit(solution)/shard_map/pallas_call | solution.py:353
  60.5 1.1 %shard_map.94 = (bf16[4,80,512]{2,1,0:T(8,128)(2,1)}, bf16[4,80,512]{2,1,0:T(8,128)(2,1)}, bf16[4,80,512]{2,1,0:T(8,128)(2,1)}, bf16[4,80,512]{2,1,0:T(8,128)(2,1)}) custom-call(bf16[4,80,512]{2,1,0:T(8,128)(2,1)S(1)} %get-tuple-element.8.refs_0_, bf16[4,80,512]{2,1,0:T(8,128)(2,1)S(1)} %get-tuple-element.9.refs_1_, ...), custom_call_target="tpu_custom_call" | custom-call | bytes 2621440 | tf_op jit(solution)/shard_map/pallas_call | solution.py:332
